TPU v7x, 512 devices: a whole 4x8x8 slice. The times are simulated.
512 devices in a mesh: section: 16 (over z, core), tensor: 16 (over y_lo, x), dp: 2 (over y_hi).
Axes of the slice: x: 4, y: 8 (y_hi: 2, y_lo: 4; y = y_hi * 4 + y_lo), z: 8, core: 2. Of those that a mesh axis runs over, the one named last changes fastest.
Arguments:
- enc_hidden: bfloat16 [512, 2048], P(('dp', 'tensor'), 'section'), parts along dimension 0, may hold values from -70 to 70
- mlp_gain: float32 [2048], P('section'), may hold values from 0.25 to 1.75
- final_gain: float32 [2048], P('section'), may hold values from 0.25 to 1.75
- w_gate: bfloat16 [2048, 8192], P('section', 'tensor'), may hold values from -0.125 to 0.125
- w_up: bfloat16 [2048, 8192], P('section', 'tensor'), may hold values from -0.125 to 0.125
- w_down: bfloat16 [8192, 2048], P('tensor', 'section'), may hold values from -0.0625 to 0.0625
- key_weight: bfloat16 [16, 2048, 4096], P('section', None, 'tensor'), may hold values from -0.125 to 0.125
- value_weight: bfloat16 [16, 2048, 4096], P('section', None, 'tensor'), may hold values from -0.125 to 0.125
- queries: bfloat16 [16, 2048, 4096], P('section', 'dp', 'tensor'), parts along dimension 1, may hold values from -340 to 340
- context_grad: bfloat16 [16, 2048, 4096], P('section', 'dp', 'tensor'), parts along dimension 1, may hold values from -6 to 6
Outputs:
- query_grad: bfloat16 [16, 2048, 4096], P('section', 'dp', 'tensor'), parts along dimension 1
- hidden_grad: float32 [512, 2048], P(('dp', 'tensor'), 'section'), parts along dimension 0
- gate_weight_grad: bfloat16 [4096, 8192], P(('dp', 'section'), 'tensor'), parts along dimension 0
- up_weight_grad: bfloat16 [4096, 8192], P(('dp', 'section'), 'tensor'), parts along dimension 0
- down_weight_grad: bfloat16 [16384, 2048], P(('dp', 'tensor'), 'section'), parts along dimension 0
There are 2 independent parts, one for each index of `dp`. A program takes and returns all parts, laid end to end along the dimension named above; an argument that names none is the same for every part. Nothing has to cross between parts.
All inputs are finite; a program needn't handle non-finite values.
Results may differ from a plain program's by a relative error of at most 0.017.
Values may be sent and summed in bfloat16 or wider, within the bound.
No kernel may reach another device: no remote copies, remote signals or barrier semaphores. Data moves between devices by JAX's collectives and lax.ppermute only.
A program may use at most 64 MiB of HBM per device.

v0:
```python
import jax
import jax.numpy as jnp
from jax import lax
from jax.sharding import PartitionSpec as P

D = 2048
HEAD = 256
EPSILON = 1e-06


def sent_to_all(value, axis):
    copies = jnp.broadcast_to(value, (lax.axis_size(axis), *value.shape))
    return lax.all_to_all(copies, axis, split_axis=0, concat_axis=0, tiled=True)


def of_everyone(value, axis):
    everything = sent_to_all(value, axis)
    return jnp.sum(everything, axis=0)


def in_order(pieces, dim):
    dims = list(pieces.shape[1:])
    dims[dim] *= pieces.shape[0]
    return jnp.moveaxis(pieces, 0, dim).reshape(dims)


def collect(value, axis, dim):
    return in_order(sent_to_all(value, axis), dim)


def in_blocks(value, dim, size):
    before, after = (value.shape[:dim], value.shape[dim + 1 :])
    return jnp.moveaxis(value.reshape(*before, size, -1, *after), dim, 0)


def summed_on_arrival(value, axis, dim):
    pieces = in_blocks(value, dim, lax.axis_size(axis))
    arrived = lax.all_to_all(pieces, axis, split_axis=0, concat_axis=0, tiled=True)
    return arrived.sum(axis=0)


def side_by_side(arrays, axis, dim, along):
    ends, at = ([], 0)
    for a in arrays[:-1]:
        at += a.shape[along]
        ends.append(at)
    both = jnp.concatenate(arrays, axis=along)
    return tuple(jnp.split(lax.all_gather(both, axis, axis=dim, tiled=True), ends, axis=along))


def attend(query_block, grad_block, keys, values):
    scale_factor = HEAD ** (-0.5)
    tgt_rows = query_block.shape[0]
    src_rows = keys.shape[0]
    heads_here = query_block.shape[1] // HEAD
    query_heads = query_block.reshape(tgt_rows, heads_here, HEAD)
    key_heads = keys.reshape(src_rows, heads_here, HEAD)
    value_heads = values.reshape(src_rows, heads_here, HEAD)
    grad_heads = grad_block.reshape(tgt_rows, heads_here, HEAD)
    scores = (
        jnp.einsum("qhd,khd->hqk", query_heads, key_heads, preferred_element_type=jnp.float32)
        * scale_factor
    )
    probs = jax.nn.softmax(scores, axis=-1)
    probs_bf = probs.astype(jnp.bfloat16)
    context = jnp.einsum("hqk,khd->qhd", probs_bf, value_heads, preferred_element_type=jnp.float32)
    delta = jnp.sum(grad_heads.astype(jnp.float32) * context, axis=2)
    dprob = jnp.einsum("qhd,khd->hqk", grad_heads, value_heads, preferred_element_type=jnp.float32)
    dscore = (probs * (dprob - jnp.transpose(delta)[:, :, None]) * scale_factor).astype(
        jnp.bfloat16
    )
    query_grad = jnp.einsum(
        "hqk,khd->qhd", dscore, key_heads, preferred_element_type=jnp.float32
    ).astype(jnp.bfloat16)
    key_grad = jnp.einsum(
        "hqk,qhd->khd", dscore, query_heads, preferred_element_type=jnp.float32
    ).astype(jnp.bfloat16)
    value_grad = jnp.einsum(
        "hqk,qhd->khd", probs_bf, grad_heads, preferred_element_type=jnp.float32
    ).astype(jnp.bfloat16)
    width = heads_here * HEAD
    return (
        query_grad.reshape(tgt_rows, width),
        key_grad.reshape(src_rows, width),
        value_grad.reshape(src_rows, width),
    )


def on_device(
    enc_hidden,
    mlp_gain,
    final_gain,
    w_gate,
    w_up,
    w_down,
    key_weight,
    value_weight,
    queries,
    context_grad,
):
    rows_contract = (((0,), (0,)), ((), ()))
    cols_contract = (((1,), (1,)), ((), ()))
    hidden_wide = enc_hidden.astype(jnp.float32)
    square_in = of_everyone(jnp.sum(hidden_wide * hidden_wide, axis=1), "section")
    inv_in = lax.rsqrt(square_in / D + EPSILON)[:, None]
    normed = (hidden_wide * inv_in * mlp_gain[None, :]).astype(jnp.bfloat16)
    normed_all = collect(normed, "tensor", 0)
    picked = normed_all
    gate_part = jnp.dot(picked, w_gate, preferred_element_type=jnp.float32)
    up_part = jnp.dot(picked, w_up, preferred_element_type=jnp.float32)
    gate_up = summed_on_arrival(jnp.concatenate([gate_part, up_part], axis=1), "section", 0)
    hidden_width = w_gate.shape[1]
    gate_pre = gate_up[:, :hidden_width]
    up_pre = gate_up[:, hidden_width:]
    sigmoid_gate = jax.nn.sigmoid(gate_pre)
    activated = gate_pre * sigmoid_gate
    hidden_act = (activated * up_pre).astype(jnp.bfloat16)
    hidden_all = collect(hidden_act, "section", 0)
    picked = hidden_all
    mixed = summed_on_arrival(
        jnp.dot(picked, w_down, preferred_element_type=jnp.float32), "tensor", 0
    )
    outer = hidden_wide + mixed
    square_out = of_everyone(jnp.sum(outer * outer, axis=1), "section")
    inv_out = lax.rsqrt(square_out / D + EPSILON)[:, None]
    encoded = (outer * inv_out * final_gain[None, :]).astype(jnp.bfloat16)
    key_matrix = key_weight[0]
    value_matrix = value_weight[0]
    head_width = key_matrix.shape[1]
    encoded_feat = lax.all_gather(encoded, "section", axis=1, tiled=True)
    block_rows = collect(encoded_feat, "tensor", 0)
    key_part = jnp.dot(block_rows, key_matrix, preferred_element_type=jnp.float32)
    value_part = jnp.dot(block_rows, value_matrix, preferred_element_type=jnp.float32)
    joined = jnp.concatenate([key_part, value_part], axis=1)
    keys_wide = joined[:, :head_width]
    values_wide = joined[:, head_width:]
    keys = keys_wide.astype(jnp.bfloat16)
    values = values_wide.astype(jnp.bfloat16)
    query_grad, key_grad, value_grad = attend(queries[0], context_grad[0], keys, values)
    total = lax.dot_general(key_grad, key_matrix, cols_contract, preferred_element_type=jnp.float32)
    partial_rows = summed_on_arrival(
        total
        + lax.dot_general(
            value_grad, value_matrix, cols_contract, preferred_element_type=jnp.float32
        ),
        "tensor",
        0,
    )
    encoded_grad = summed_on_arrival(partial_rows, "section", 1)
    scaled_out = final_gain[None, :] * encoded_grad
    inner_out = of_everyone(jnp.sum(scaled_out * outer, axis=1), "section")
    outer_grad = (
        inv_out * scaled_out - outer * inv_out * inv_out * inv_out * (inner_out / D)[:, None]
    )
    outer_grad_bf = outer_grad.astype(jnp.bfloat16)
    outer_all = collect(outer_grad_bf, "tensor", 0)
    down_weight_grad = lax.dot_general(
        hidden_all, outer_all, rows_contract, preferred_element_type=jnp.float32
    ).astype(jnp.bfloat16)
    picked = outer_all
    act_grad = summed_on_arrival(
        lax.dot_general(picked, w_down, cols_contract, preferred_element_type=jnp.float32),
        "section",
        0,
    )
    up_grad = (act_grad * activated).astype(jnp.bfloat16)
    gate_grad = (act_grad * up_pre * sigmoid_gate * (1.0 + gate_pre * (1.0 - sigmoid_gate))).astype(
        jnp.bfloat16
    )
    gate_all, up_all = side_by_side((gate_grad, up_grad), "section", 0, 1)
    gate_weight_grad = lax.dot_general(
        normed_all, gate_all, rows_contract, preferred_element_type=jnp.float32
    ).astype(jnp.bfloat16)
    up_weight_grad = lax.dot_general(
        normed_all, up_all, rows_contract, preferred_element_type=jnp.float32
    ).astype(jnp.bfloat16)
    total = lax.dot_general(gate_all, w_gate, cols_contract, preferred_element_type=jnp.float32)
    normed_grad = summed_on_arrival(
        total + lax.dot_general(up_all, w_up, cols_contract, preferred_element_type=jnp.float32),
        "tensor",
        0,
    )
    scaled_in = mlp_gain[None, :] * normed_grad
    inner_in = of_everyone(jnp.sum(scaled_in * hidden_wide, axis=1), "section")
    hidden_grad = (
        outer_grad
        + inv_in * scaled_in
        - hidden_wide * inv_in * inv_in * inv_in * (inner_in / D)[:, None]
    )
    return (query_grad[None, :, :], hidden_grad, gate_weight_grad, up_weight_grad, down_weight_grad)


def solution(mesh):
    in_specs = (
        P(("dp", "tensor"), "section"),
        P("section"),
        P("section"),
        P("section", "tensor"),
        P("section", "tensor"),
        P("tensor", "section"),
        P("section", None, "tensor"),
        P("section", None, "tensor"),
        P("section", "dp", "tensor"),
        P("section", "dp", "tensor"),
    )
    out_specs = (
        P("section", "dp", "tensor"),
        P(("dp", "tensor"), "section"),
        P(("dp", "section"), "tensor"),
        P(("dp", "section"), "tensor"),
        P(("dp", "tensor"), "section"),
    )
    return jax.shard_map(
        on_device, mesh=mesh, in_specs=in_specs, out_specs=out_specs, check_vma=False
    )
```

profile of v0, /device:TPU:1, one launch (start us, length us, event | category | flops | bytes accessed | tf_op | source)
XLA Modules:
  0.0 323.9 jit_solution(14428593524110861365)
XLA Ops:
  0.6 0.0 copy-start
  0.6 0.9 fusion.37
  1.5 18.6 %all_to_all.74 = f32[16,1,16]{2,1,0:T(1,128)S(1)} all-to-all(f32[16,1,16]{2,1,0:T(1,128)S(1)} %broadcast_in_dim.16), channel_id=1, replica_groups=mesh['section'=16,'tensor'=16,'dp'=2] {'section'}, dimensions={0} | all-to-all | bytes 2048 | tf_op jit(solution)/shard_map/all_to_all | solution.py:13
  20.2 0.5 copy-done.19
  20.7 0.8 fusion.33
  21.5 14.2 %all_to_all.75 = bf16[16,16,128]{2,1,0:T(8,128)(2,1)S(1)} all-to-all(bf16[16,16,128]{2,1,0:T(8,128)(2,1)S(1)} %broadcast_in_dim.17), channel_id=1, replica_groups=mesh['section'=16,'tensor'=16,'dp'=2] {'tensor'}, dimensions={0} | all-to-all | bytes 131072 | tf_op jit(solution)/shard_map/all_to_all | solution.py:13
  35.7 1.1 fusion.45
  36.8 1.1 fusion.44
  37.9 0.1 pad_maximum_fusion
  38.0 0.0 copy-start.11
  38.1 0.0 copy-start.14
  38.1 33.2 %all_to_all.76 = f32[16,16,1024]{2,1,0:T(8,128)S(1)} all-to-all(f32[16,16,1024]{2,1,0:T(8,128)S(1)} %bitcast.86), channel_id=1, replica_groups=mesh['section'=16,'tensor'=16,'dp'=2] {'section'}, dimensions={0} | all-to-all | bytes 2097152 | tf_op jit(solution)/shard_map/all_to_all | solution.py:38
  71.3 0.1 reduce_sum.146
  71.4 14.4 %all_to_all.77 = bf16[16,16,512]{2,1,0:T(8,128)(2,1)S(1)} all-to-all(bf16[16,16,512]{2,1,0:T(8,128)(2,1)S(1)} %broadcast_in_dim.36), channel_id=1, replica_groups=mesh['section'=16,'tensor'=16,'dp'=2] {'section'}, dimensions={0} | all-to-all | bytes 524288 | tf_op jit(solution)/shard_map/all_to_all | solution.py:13
  85.8 0.7 copy-done.5
  86.6 0.2 fusion.28
  86.8 11.7 %all_to_all.78 = f32[16,16,128]{2,1,0:T(8,128)S(1)} all-to-all(f32[16,16,128]{2,1,0:T(8,128)S(1)} %fusion.28), channel_id=1, replica_groups=mesh['section'=16,'tensor'=16,'dp'=2] {'tensor'}, dimensions={0} | all-to-all | bytes 262144 | tf_op jit(solution)/shard_map/all_to_all | solution.py:38
  98.5 0.1 multiply_reduce_fusion.1
  98.6 9.9 %all_to_all.79 = f32[16,1,16]{2,1,0:T(1,128)S(1)} all-to-all(f32[16,1,16]{2,1,0:T(1,128)S(1)} %broadcast_in_dim.37), channel_id=1, replica_groups=mesh['section'=16,'tensor'=16,'dp'=2] {'section'}, dimensions={0} | all-to-all | bytes 2048 | tf_op jit(solution)/shard_map/all_to_all | solution.py:13
  108.5 0.1 multiply_convert_fusion.3
  108.6 15.3 %all_gather.6 = bf16[16,2048]{1,0:T(8,128)(2,1)S(1)} all-gather(bf16[16,128]{1,0:T(8,128)(2,1)S(1)} %multiply_convert_fusion.3), channel_id=1, replica_groups=mesh['section'=16,'tensor'=16,'dp'=2] {'section'}, dimensions={1}, use_global_device_ids=true | all-gather | bytes 69632 | tf_op jit(solution)/shard_map/all_gather | solution.py:130
  124.0 1.1 broadcast_in_dim.38
  125.1 3.7 %all-to-all-start.6 = ((bf16[16,16,2048]{2,1,0:T(8,128)(2,1)}), bf16[16,16,2048]{2,1,0:T(8,128)(2,1)S(1)}, u32[]{:S(2)}, u32[]{:S(2)}) async-start(bf16[16,16,2048]{2,1,0:T(8,128)(2,1)} %broadcast_in_dim.38), calls=%async_computation.6 | async-start | bytes 2097152 | tf_op jit(solution)/shard_map/all_to_all | solution.py:13
  128.7 2.0 copy.27
  130.8 21.3 %all-to-all-done.6 = bf16[16,16,2048]{2,1,0:T(8,128)(2,1)S(1)} async-done(((bf16[16,16,2048]{2,1,0:T(8,128)(2,1)}), bf16[16,16,2048]{2,1,0:T(8,128)(2,1)S(1)}, u32[]{:S(2)}, u32[]{:S(2)}) %all-to-all-start.6) | async-done | bytes 1048608 | tf_op jit(solution)/shard_map/all_to_all | solution.py:13
  152.1 0.4 convolution_convert_fusion.5
  152.6 0.0 copy-start.7
  152.6 0.4 convolution_convert_fusion.6
  153.0 0.1 copy-done.2
  153.2 0.3 fusion.43
  153.5 0.2 fusion.13
  153.7 0.0 copy-start.12
  153.7 0.0 copy-start.3
  153.7 0.4 fusion.4
  154.1 0.2 copy-done.12
  154.3 0.5 copy-done.3
  154.7 1.2 fusion.3
  155.9 3.5 %fusion.7 = f32[256,2048]{1,0:T(8,128)} fusion(bf16[256,1024]{1,0:T(8,128)(2,1)} %fusion.3, bf16[1,2048,256]{2,1,0:T(8,128)(2,1)S(1)} %copy-done, bf16[1,1024,256]{2,1,0:T(8,128)(2,1)} %param.18), kind=kOutput, calls=%fused_computation.20 | convolution fusion | flops 402718720 | bytes 4194304 | tf_op jit(solution)/shard_map/dot_general | solution.py:140
  159.4 4.0 %convolution_add_fusion = f32[256,2048]{1,0:T(8,128)} fusion(f32[256,2048]{1,0:T(8,128)} %fusion.7, bf16[1,2048,256]{2,1,0:T(8,128)(2,1)S(1)} %copy-done.1, bf16[1,1024,256]{2,1,0:T(8,128)(2,1)} %param.19, f32[1024]{0:T(1024)S(1)} %copy-done.13, f32[256,1024]{1,0:T(8,128)S(1)} %get-tuple-element.33, f32[1024]{0:T(1024)S(1)} %get-tuple-element.32), kind=kOutput, calls=%fused_computation | convolution fusion | flops 404029440 | bytes 6823936 | tf_op jit(solution)/shard_map/dot_general | solution.py:143
  163.4 54.4 %all_to_all.80 = f32[16,16,2048]{2,1,0:T(8,128)S(1)} all-to-all(f32[16,16,2048]{2,1,0:T(8,128)} %bitcast.85), channel_id=1, replica_groups=mesh['section'=16,'tensor'=16,'dp'=2] {'tensor'}, dimensions={0} | all-to-all | bytes 4194304 | tf_op jit(solution)/shard_map/all_to_all | solution.py:38
  217.8 0.1 reduce_sum.152
  218.0 15.9 %all_to_all.81 = f32[16,16,128]{2,1,0:T(8,128)S(1)} all-to-all(f32[16,16,128]{2,1,0:T(8,128)S(1)} %copy.28), channel_id=1, replica_groups=mesh['section'=16,'tensor'=16,'dp'=2] {'section'}, dimensions={0} | all-to-all | bytes 262144 | tf_op jit(solution)/shard_map/all_to_all | solution.py:38
  234.0 0.1 multiply_reduce_fusion
  234.1 9.4 %all_to_all.82 = f32[16,1,16]{2,1,0:T(1,128)S(1)} all-to-all(f32[16,1,16]{2,1,0:T(1,128)S(1)} %broadcast_in_dim.39), channel_id=1, replica_groups=mesh['section'=16,'tensor'=16,'dp'=2] {'section'}, dimensions={0} | all-to-all | bytes 2048 | tf_op jit(solution)/shard_map/all_to_all | solution.py:13
  243.6 0.7 fusion.39
  244.3 11.2 %all_to_all.83 = bf16[16,16,128]{2,1,0:T(8,128)(2,1)S(1)} all-to-all(bf16[16,16,128]{2,1,0:T(8,128)(2,1)S(1)} %broadcast_in_dim.40), channel_id=1, replica_groups=mesh['section'=16,'tensor'=16,'dp'=2] {'tensor'}, dimensions={0} | all-to-all | bytes 131072 | tf_op jit(solution)/shard_map/all_to_all | solution.py:13
  255.5 1.9 fusion.26
  257.4 5.6 %all-to-all-start.11 = ((f32[16,16,512]{2,1,0:T(8,128)}), f32[16,16,512]{2,1,0:T(8,128)S(1)}, u32[]{:S(2)}, u32[]{:S(2)}) async-start(f32[16,16,512]{2,1,0:T(8,128)} %fusion.26), calls=%async_computation.11 | async-start | bytes 1048576 | tf_op jit(solution)/shard_map/all_to_all | solution.py:38
  263.0 0.3 fusion.5
  263.4 1.0 copy.31
  264.4 16.0 %all-to-all-done.11 = f32[16,16,512]{2,1,0:T(8,128)S(1)} async-done(((f32[16,16,512]{2,1,0:T(8,128)}), f32[16,16,512]{2,1,0:T(8,128)S(1)}, u32[]{:S(2)}, u32[]{:S(2)}) %all-to-all-start.11) | async-done | bytes 524320 | tf_op jit(solution)/shard_map/all_to_all | solution.py:38
  280.4 15.9 %all_gather.7 = bf16[256,1024]{1,0:T(8,128)(2,1)S(1)} all-gather(bf16[16,1024]{1,0:T(8,128)(2,1)S(1)} %pad_maximum_fusion.1), channel_id=1, replica_groups=mesh['section'=16,'tensor'=16,'dp'=2] {'section'}, dimensions={0}, use_global_device_ids=true | all-gather | bytes 557056 | tf_op jit(solution)/shard_map/all_gather | solution.py:48
  296.4 0.2 fusion.24
  296.6 0.9 convolution_add_fusion.1
  297.5 3.5 %all-to-all-start.12 = ((f32[16,16,128]{2,1,0:T(8,128)}), f32[16,16,128]{2,1,0:T(8,128)S(1)}, u32[]{:S(2)}, u32[]{:S(2)}) async-start(f32[16,16,128]{2,1,0:T(8,128)} %bitcast.19), calls=%async_computation.12 | async-start | bytes 262144 | tf_op jit(solution)/shard_map/all_to_all | solution.py:38
  301.0 0.9 fusion.6
  301.9 0.9 convolution_convert_fusion.4
  302.8 6.4 %all-to-all-done.12 = f32[16,16,128]{2,1,0:T(8,128)S(1)} async-done(((f32[16,16,128]{2,1,0:T(8,128)}), f32[16,16,128]{2,1,0:T(8,128)S(1)}, u32[]{:S(2)}, u32[]{:S(2)}) %all-to-all-start.12) | async-done | bytes 131104 | tf_op jit(solution)/shard_map/all_to_all | solution.py:38
  309.3 0.1 fusion.38
  309.4 0.6 broadcast_in_dim.41
  310.0 6.2 %all-to-all-start.13 = ((f32[16,1,16]{2,1,0:T(1,128)}), f32[16,1,16]{2,1,0:T(1,128)S(1)}, u32[]{:S(2)}, u32[]{:S(2)}) async-start(f32[16,1,16]{2,1,0:T(1,128)} %broadcast_in_dim.41), calls=%async_computation.13 | async-start | bytes 16384 | tf_op jit(solution)/shard_map/all_to_all | solution.py:13
  316.2 0.9 convolution_convert_fusion.3
  317.1 6.1 %all-to-all-done.13 = f32[16,1,16]{2,1,0:T(1,128)S(1)} async-done(((f32[16,1,16]{2,1,0:T(1,128)}), f32[16,1,16]{2,1,0:T(1,128)S(1)}, u32[]{:S(2)}, u32[]{:S(2)}) %all-to-all-start.13) | async-done | bytes 1056 | tf_op jit(solution)/shard_map/all_to_all | solution.py:13
  323.2 0.7 fusion.36
  (54 shorter events, 0.5 us)
Async XLA Ops:
  0.6 151.9 %copy-start = (bf16[1,2048,256]{2,1,0:T(8,128)(2,1)S(1)}, bf16[1,2048,256]{2,1,0:T(8,128)(2,1)}, u32[]{:S(2)}) copy-start(bf16[1,2048,256]{2,1,0:T(8,128)(2,1)} %param.16) | copy-start | bytes 3145732
  20.2 0.5 copy-start.19
  38.0 48.5 %copy-start.9 = (bf16[512,128]{1,0:T(8,128)(2,1)S(1)}, bf16[512,128]{1,0:T(8,128)(2,1)}, u32[]{:S(2)}) copy-start(bf16[512,128]{1,0:T(8,128)(2,1)} %param.15) | copy-start | bytes 393220
  38.0 60.5 %copy-start.11 = (bf16[16,128]{1,0:T(8,128)(2,1)S(1)}, bf16[16,128]{1,0:T(8,128)(2,1)}, u32[]{:S(2)}) copy-start(bf16[16,128]{1,0:T(8,128)(2,1)} %param.10) | copy-start | bytes 12292
  38.1 70.5 %copy-start.14 = (f32[128]{0:T(128)S(1)}, f32[128]{0:T(128)}, u32[]{:S(2)}) copy-start(f32[128]{0:T(128)} %param.12) | copy-start | bytes 1540
  85.8 0.7 copy-start.5
  108.5 22.2 %copy-start.16 = (f32[16]{0:T(128)}, f32[16]{0:T(128)S(1)}, u32[]{:S(2)}) copy-start(f32[16]{0:T(128)S(1)} %add_rsqrt_fusion) | copy-start | bytes 196
  123.9 28.2 %copy-start.1 = (bf16[1,2048,256]{2,1,0:T(8,128)(2,1)S(1)}, bf16[1,2048,256]{2,1,0:T(8,128)(2,1)}, u32[]{:S(2)}) copy-start(bf16[1,2048,256]{2,1,0:T(8,128)(2,1)} %param.17) | copy-start | bytes 3145732
  125.1 27.1 %all-to-all-start.6 = ((bf16[16,16,2048]{2,1,0:T(8,128)(2,1)}), bf16[16,16,2048]{2,1,0:T(8,128)(2,1)S(1)}, u32[]{:S(2)}, u32[]{:S(2)}) async-start(bf16[16,16,2048]{2,1,0:T(8,128)(2,1)} %broadcast_in_dim.38), calls=%async_computation.6 | async-start | bytes 2097152 | tf_op jit(solution)/shard_map/all_to_all | solution.py:13
  152.1 1.0 copy-start.2
  152.6 1.1 copy-start.7
  153.7 0.6 copy-start.12
  153.7 1.0 copy-start.3
  155.9 3.5 %copy-start.13 = (f32[1024]{0:T(1024)S(1)}, f32[1024]{0:T(1024)}, u32[]{:S(2)}) copy-start(f32[1024]{0:T(1024)} %copy-done.12) | copy-start | bytes 12292
  217.8 16.2 %copy-start.15 = (f32[128]{0:T(128)S(1)}, f32[128]{0:T(128)}, u32[]{:S(2)}) copy-start(f32[128]{0:T(128)} %param.12) | copy-start | bytes 1540
  217.9 45.1 %copy-start.4 = (bf16[256,1024]{1,0:T(8,128)(2,1)S(1)}, bf16[256,1024]{1,0:T(8,128)(2,1)}, u32[]{:S(2)}) copy-start(bf16[256,1024]{1,0:T(8,128)(2,1)} %fusion.3) | copy-start | bytes 1572868
  257.4 38.9 %copy-start.10 = (bf16[128,512]{1,0:T(8,128)(2,1)S(1)}, bf16[128,512]{1,0:T(8,128)(2,1)}, u32[]{:S(2)}) copy-start(bf16[128,512]{1,0:T(8,128)(2,1)} %param.13) | copy-start | bytes 393220
  257.4 22.9 %all-to-all-start.11 = ((f32[16,16,512]{2,1,0:T(8,128)}), f32[16,16,512]{2,1,0:T(8,128)S(1)}, u32[]{:S(2)}, u32[]{:S(2)}) async-start(f32[16,16,512]{2,1,0:T(8,128)} %fusion.26), calls=%async_computation.11 | async-start | bytes 1048576 | tf_op jit(solution)/shard_map/all_to_all | solution.py:38
  263.0 33.6 %copy-start.8 = (bf16[128,512]{1,0:T(8,128)(2,1)S(1)}, bf16[128,512]{1,0:T(8,128)(2,1)}, u32[]{:S(2)}) copy-start(bf16[128,512]{1,0:T(8,128)(2,1)} %param.14) | copy-start | bytes 393220
  263.3 37.7 %copy-start.6 = (bf16[16,16,512]{2,1,0:T(8,128)(2,1)S(1)}, bf16[16,16,512]{2,1,0:T(8,128)(2,1)}, u32[]{:S(2)}) copy-start(bf16[16,16,512]{2,1,0:T(8,128)(2,1)} %copy-done.5) | copy-start | bytes 786436
  280.4 28.8 %copy-start.18 = (f32[128]{0:T(128)S(1)}, f32[128]{0:T(128)}, u32[]{:S(2)}) copy-start(f32[128]{0:T(128)} %param.11) | copy-start | bytes 1540
  296.4 26.8 %copy-start.17 = (f32[16]{0:T(128)S(1)}, f32[16]{0:T(128)}, u32[]{:S(2)}) copy-start(f32[16]{0:T(128)} %copy-done.16) | copy-start | bytes 196
  296.4 26.8 %copy-start.20 = (f32[16]{0:T(128)S(1)}, f32[16]{0:T(128)}, u32[]{:S(2)}) copy-start(f32[16]{0:T(128)} %copy-done.19) | copy-start | bytes 196
  297.5 11.7 %all-to-all-start.12 = ((f32[16,16,128]{2,1,0:T(8,128)}), f32[16,16,128]{2,1,0:T(8,128)S(1)}, u32[]{:S(2)}, u32[]{:S(2)}) async-start(f32[16,16,128]{2,1,0:T(8,128)} %bitcast.19), calls=%async_computation.12 | async-start | bytes 262144 | tf_op jit(solution)/shard_map/all_to_all | solution.py:38
  310.0 13.2 %all-to-all-start.13 = ((f32[16,1,16]{2,1,0:T(1,128)}), f32[16,1,16]{2,1,0:T(1,128)S(1)}, u32[]{:S(2)}, u32[]{:S(2)}) async-start(f32[16,1,16]{2,1,0:T(1,128)} %broadcast_in_dim.41), calls=%async_computation.13 | async-start | bytes 16384 | tf_op jit(solution)/shard_map/all_to_all | solution.py:13
where the time goes:
time: 325 us; the launch traced here: 324 us
  blocking collectives  224 us (69%)
  waiting for transfers between devices  49.8 us (15%)
  starting transfers between devices  19 us (6%)
  matrix products  18.7 us (6%)
  local copies, waits for them, and re-layouts  7 us (2%)
  other arithmetic  4.11 us (1%)
    all_to_all x4, blocking collectives, summed_on_arrival(): lax.all_to_all(pieces, axis, split_axis=0, concat_axis=0, tiled=True)  115 us
    all_to_all x6, blocking collectives, sent_to_all(): return lax.all_to_all(copies, axis, split_axis=0, concat_axis=0, tiled=True)  77.8 us
    all_to_all x2, waiting for transfers between devices, sent_to_all(): return lax.all_to_all(copies, axis, split_axis=0, concat_axis=0, tiled=True)  27.4 us
    all_to_all x2, waiting for transfers between devices, summed_on_arrival(): lax.all_to_all(pieces, axis, split_axis=0, concat_axis=0, tiled=True)  22.4 us
    all_gather x1, blocking collectives, side_by_side(): lax.all_gather(both, axis, axis=dim, tiled=True)  15.9 us
    all_gather x1, blocking collectives, on_device(): encoded_feat = lax.all_gather(encoded, 'section', axis=1, tiled=True)  15.3 us
    all_to_all x2, starting transfers between devices, sent_to_all(): return lax.all_to_all(copies, axis, split_axis=0, concat_axis=0, tiled=True)  9.87 us
    all_to_all x2, starting transfers between devices, summed_on_arrival(): lax.all_to_all(pieces, axis, split_axis=0, concat_axis=0, tiled=True)  9.09 us
  transfers between devices with their start and end apart: 4, of which 4 were waited for; matrix products, arithmetic and copies ran while one was open for 2% of the time, Pallas kernels for 0%

commit v1 on v0

--- a/solution.py
+++ b/solution.py
@@ -6,6 +6,22 @@
 D = 2048
 HEAD = 256
 EPSILON = 1e-06
+
+
+def gather_around(x, axis, dim):
+    ways, here, hop = (lax.axis_size(axis), lax.axis_index(axis), x.shape[dim])
+    dims = [n * ways if d == dim else n for d, n in enumerate(x.shape)]
+    full = lax.dynamic_update_slice_in_dim(jnp.zeros(dims, x.dtype), x, here * hop, axis=dim)
+    going_up = going_down = x
+    for far in range(1, ways // 2 + 1):
+        going_up = lax.ppermute(going_up, axis, [(d, (d + 1) % ways) for d in range(ways)])
+        full = lax.dynamic_update_slice_in_dim(full, going_up, (here - far) % ways * hop, axis=dim)
+        if 2 * far < ways:
+            going_down = lax.ppermute(going_down, axis, [(d, (d - 1) % ways) for d in range(ways)])
+            full = lax.dynamic_update_slice_in_dim(
+                full, going_down, (here + far) % ways * hop, axis=dim
+            )
+    return full
 
 
 def sent_to_all(value, axis):
@@ -127,7 +143,7 @@
     key_matrix = key_weight[0]
     value_matrix = value_weight[0]
     head_width = key_matrix.shape[1]
-    encoded_feat = lax.all_gather(encoded, "section", axis=1, tiled=True)
+    encoded_feat = gather_around(encoded, "section", 1)
     block_rows = collect(encoded_feat, "tensor", 0)
     key_part = jnp.dot(block_rows, key_matrix, preferred_element_type=jnp.float32)
     value_part = jnp.dot(block_rows, value_matrix, preferred_element_type=jnp.float32)

time: 325 us -> 342 us (1.052)
  blocking collectives: 224 us -> 188 us
  starting transfers between devices: 19 us -> 47 us
  waiting for transfers between devices: 49.8 us -> 73.7 us
    ppermute x0 -> x15, starting transfers between devices: none -> 20.8 us  [the longest x7 16.3 us: gather_around(): lax.ppermute(going_down, axis, [(d, (d - 1) % ways) for d in range(ways)])]
    all_gather x1 -> x0, blocking collectives: 15.3 us -> none  [on_device(): encoded_feat = lax.all_gather(encoded, 'section', axis=1, tiled=True)]
    all_to_all x4 -> x3, blocking collectives: 115 us -> 103 us  [summed_on_arrival(): lax.all_to_all(pieces, axis, split_axis=0, concat_axis=0, tiled=True)]
    ppermute x0 -> x15, waiting for transfers between devices: none -> 10.1 us  [the longest x8 8.36 us: gather_around(): lax.ppermute(going_up, axis, [(d, (d + 1) % ways) for d in range(ways)])]
    all_to_all x6 -> x5, blocking collectives: 77.8 us -> 68.6 us  [sent_to_all(): return lax.all_to_all(copies, axis, split_axis=0, concat_axis=0, tiled=True)]
    all_to_all x2 -> x3, waiting for transfers between devices: 22.4 us -> 31.3 us  [summed_on_arrival(): lax.all_to_all(pieces, axis, split_axis=0, concat_axis=0, tiled=True)]
    all_to_all x2 -> x3, waiting for transfers between devices: 27.4 us -> 32.3 us  [sent_to_all(): return lax.all_to_all(copies, axis, split_axis=0, concat_axis=0, tiled=True)]
    all_to_all x2 -> x3, starting transfers between devices: 9.87 us -> 13.6 us  [sent_to_all(): return lax.all_to_all(copies, axis, split_axis=0, concat_axis=0, tiled=True)]
  transfers between devices with their start and end apart: 4 -> 21, of which waited for: 4 -> 21; matrix products, arithmetic and copies ran while one was open for 2% -> 2% of each run, Pallas kernels for 0% -> 0%
where the time goes in v1:
time: 342 us; the launch traced here: 341 us
  blocking collectives  188 us (55%)
  waiting for transfers between devices  73.7 us (22%)
  starting transfers between devices  47 us (14%)
  matrix products  19.3 us (6%)
  local copies, waits for them, and re-layouts  7.75 us (2%)
  other arithmetic  4.19 us (1%)
    all_to_all x3, blocking collectives, summed_on_arrival(): lax.all_to_all(pieces, axis, split_axis=0, concat_axis=0, tiled=True)  103 us
    all_to_all x5, blocking collectives, sent_to_all(): return lax.all_to_all(copies, axis, split_axis=0, concat_axis=0, tiled=True)  68.6 us
    all_to_all x3, waiting for transfers between devices, sent_to_all(): return lax.all_to_all(copies, axis, split_axis=0, concat_axis=0, tiled=True)  32.3 us
    all_to_all x3, waiting for transfers between devices, summed_on_arrival(): lax.all_to_all(pieces, axis, split_axis=0, concat_axis=0, tiled=True)  31.3 us
    ppermute x7, starting transfers between devices, gather_around(): lax.ppermute(going_down, axis, [(d, (d - 1) % ways) for d in range(ways)])  16.3 us
    all_gather x1, blocking collectives, side_by_side(): lax.all_gather(both, axis, axis=dim, tiled=True)  15.9 us
    all_to_all x3, starting transfers between devices, sent_to_all(): return lax.all_to_all(copies, axis, split_axis=0, concat_axis=0, tiled=True)  13.6 us
    all_to_all x3, starting transfers between devices, summed_on_arrival(): lax.all_to_all(pieces, axis, split_axis=0, concat_axis=0, tiled=True)  12.6 us
  transfers between devices with their start and end apart: 21, of which 21 were waited for; matrix products, arithmetic and copies ran while one was open for 2% of the time, Pallas kernels for 0%

profile of v1, /device:TPU:1, one launch (start us, length us, event | category | flops | bytes accessed | tf_op | source)
XLA Modules:
  0.0 340.7 jit_solution(14773311038308597548)
XLA Ops:
  0.6 0.9 fusion.37
  1.5 18.6 %all_to_all.74 = f32[16,1,16]{2,1,0:T(1,128)S(1)} all-to-all(f32[16,1,16]{2,1,0:T(1,128)S(1)} %broadcast_in_dim.38), channel_id=1, replica_groups=mesh['section'=16,'tensor'=16,'dp'=2] {'section'}, dimensions={0} | all-to-all | bytes 2048 | tf_op jit(solution)/shard_map/all_to_all | solution.py:29
  20.2 0.5 copy-done.19
  20.7 0.8 fusion.33
  21.5 14.2 %all_to_all.75 = bf16[16,16,128]{2,1,0:T(8,128)(2,1)S(1)} all-to-all(bf16[16,16,128]{2,1,0:T(8,128)(2,1)S(1)} %broadcast_in_dim.39), channel_id=1, replica_groups=mesh['section'=16,'tensor'=16,'dp'=2] {'tensor'}, dimensions={0} | all-to-all | bytes 131072 | tf_op jit(solution)/shard_map/all_to_all | solution.py:29
  35.7 1.1 fusion.45
  36.8 1.1 fusion.44
  38.1 33.2 %all_to_all.76 = f32[16,16,1024]{2,1,0:T(8,128)S(1)} all-to-all(f32[16,16,1024]{2,1,0:T(8,128)S(1)} %bitcast.86), channel_id=1, replica_groups=mesh['section'=16,'tensor'=16,'dp'=2] {'section'}, dimensions={0} | all-to-all | bytes 2097152 | tf_op jit(solution)/shard_map/all_to_all | solution.py:54
  71.4 14.4 %all_to_all.77 = bf16[16,16,512]{2,1,0:T(8,128)(2,1)S(1)} all-to-all(bf16[16,16,512]{2,1,0:T(8,128)(2,1)S(1)} %broadcast_in_dim.40), channel_id=1, replica_groups=mesh['section'=16,'tensor'=16,'dp'=2] {'section'}, dimensions={0} | all-to-all | bytes 524288 | tf_op jit(solution)/shard_map/all_to_all | solution.py:29
  85.8 0.7 copy-done.5
  86.6 0.9 fusion.28
  87.5 3.5 %all-to-all-start.4 = ((f32[16,16,128]{2,1,0:T(8,128)}), f32[16,16,128]{2,1,0:T(8,128)S(1)}, u32[]{:S(2)}, u32[]{:S(2)}) async-start(f32[16,16,128]{2,1,0:T(8,128)} %fusion.28), calls=%async_computation.4 | async-start | bytes 262144 | tf_op jit(solution)/shard_map/all_to_all | solution.py:54
  91.1 8.9 %all-to-all-done.4 = f32[16,16,128]{2,1,0:T(8,128)S(1)} async-done(((f32[16,16,128]{2,1,0:T(8,128)}), f32[16,16,128]{2,1,0:T(8,128)S(1)}, u32[]{:S(2)}, u32[]{:S(2)}) %all-to-all-start.4) | async-done | bytes 131104 | tf_op jit(solution)/shard_map/all_to_all | solution.py:54
  100.2 0.6 broadcast_in_dim.41
  100.8 3.7 %all-to-all-start.5 = ((f32[16,1,16]{2,1,0:T(1,128)}), f32[16,1,16]{2,1,0:T(1,128)S(1)}, u32[]{:S(2)}, u32[]{:S(2)}) async-start(f32[16,1,16]{2,1,0:T(1,128)} %broadcast_in_dim.41), calls=%async_computation.5 | async-start | bytes 16384 | tf_op jit(solution)/shard_map/all_to_all | solution.py:29
  104.5 7.0 %all-to-all-done.5 = f32[16,1,16]{2,1,0:T(1,128)S(1)} async-done(((f32[16,1,16]{2,1,0:T(1,128)}), f32[16,1,16]{2,1,0:T(1,128)S(1)}, u32[]{:S(2)}, u32[]{:S(2)}) %all-to-all-start.5) | async-done | bytes 1056 | tf_op jit(solution)/shard_map/all_to_all | solution.py:29
  111.6 0.8 collective-permute-start
  112.4 0.8 collective-permute-done
  113.2 2.3 collective-permute-start.2
  115.8 0.8 collective-permute-start.3
  116.6 0.6 collective-permute-done.2
  117.2 1.3 collective-permute-start.4
  118.8 2.0 collective-permute-start.5
  120.8 0.6 collective-permute-done.4
  121.8 3.2 collective-permute-start.7
  125.1 0.6 collective-permute-done.6
  125.9 3.4 %collective-permute-start.9 = (bf16[16,128]{1,0:T(8,128)(2,1)S(1)}, bf16[16,128]{1,0:T(8,128)(2,1)S(1)}, u32[]{:S(2)}, u32[]{:S(2)}) collective-permute-start(bf16[16,128]{1,0:T(8,128)(2,1)S(1)} %collective-permute-done.7), channel_id=1, source_target_pairs={{0,480},{32,0},{64,32},{96,64},{128,96},{160,128},{192,160},{224,1... | collective-permute-start | bytes 12296 | tf_op jit(solution)/shard_map/ppermute | solution.py:20
  129.3 0.6 collective-permute-done.8
  130.1 3.4 %collective-permute-start.11 = (bf16[16,128]{1,0:T(8,128)(2,1)S(1)}, bf16[16,128]{1,0:T(8,128)(2,1)S(1)}, u32[]{:S(2)}, u32[]{:S(2)}) collective-permute-start(bf16[16,128]{1,0:T(8,128)(2,1)S(1)} %collective-permute-done.9), channel_id=1, source_target_pairs={{0,480},{32,0},{64,32},{96,64},{128,96},{160,128},{192,160},{224,1... | collective-permute-start | bytes 12296 | tf_op jit(solution)/shard_map/ppermute | solution.py:20
  133.6 0.6 collective-permute-done.10
  134.4 3.4 %collective-permute-start.13 = (bf16[16,128]{1,0:T(8,128)(2,1)S(1)}, bf16[16,128]{1,0:T(8,128)(2,1)S(1)}, u32[]{:S(2)}, u32[]{:S(2)}) collective-permute-start(bf16[16,128]{1,0:T(8,128)(2,1)S(1)} %collective-permute-done.11), channel_id=1, source_target_pairs={{0,480},{32,0},{64,32},{96,64},{128,96},{160,128},{192,160},{224,1... | collective-permute-start | bytes 12296 | tf_op jit(solution)/shard_map/ppermute | solution.py:20
  137.8 0.6 collective-permute-done.12
  138.6 4.0 %collective-permute-done.14 = bf16[16,128]{1,0:T(8,128)(2,1)S(1)} collective-permute-done((bf16[16,128]{1,0:T(8,128)(2,1)S(1)}, bf16[16,128]{1,0:T(8,128)(2,1)S(1)}, u32[]{:S(2)}, u32[]{:S(2)}) %collective-permute-start.14) | collective-permute-done | bytes 4128 | tf_op jit(solution)/shard_map/ppermute | solution.py:17
  142.7 1.1 broadcast_in_dim.42
  143.8 3.7 %all-to-all-start.6 = ((bf16[16,16,2048]{2,1,0:T(8,128)(2,1)}), bf16[16,16,2048]{2,1,0:T(8,128)(2,1)S(1)}, u32[]{:S(2)}, u32[]{:S(2)}) async-start(bf16[16,16,2048]{2,1,0:T(8,128)(2,1)} %broadcast_in_dim.42), calls=%async_computation.6 | async-start | bytes 2097152 | tf_op jit(solution)/shard_map/all_to_all | solution.py:29
  147.4 2.0 copy.27
  149.5 19.2 %all-to-all-done.6 = bf16[16,16,2048]{2,1,0:T(8,128)(2,1)S(1)} async-done(((bf16[16,16,2048]{2,1,0:T(8,128)(2,1)}), bf16[16,16,2048]{2,1,0:T(8,128)(2,1)S(1)}, u32[]{:S(2)}, u32[]{:S(2)}) %all-to-all-start.6) | async-done | bytes 1048608 | tf_op jit(solution)/shard_map/all_to_all | solution.py:29
  168.7 0.4 convolution_convert_fusion.5
  169.2 0.4 convolution_convert_fusion.6
  170.3 0.4 fusion.4
  170.9 0.5 copy-done.3
  171.3 1.2 fusion.3
  172.5 3.4 %fusion.7 = f32[256,2048]{1,0:T(8,128)} fusion(bf16[256,1024]{1,0:T(8,128)(2,1)} %fusion.3, bf16[1,2048,256]{2,1,0:T(8,128)(2,1)S(1)} %copy-done, bf16[1,1024,256]{2,1,0:T(8,128)(2,1)} %param.18), kind=kOutput, calls=%fused_computation.20 | convolution fusion | flops 402718720 | bytes 4194304 | tf_op jit(solution)/shard_map/dot_general | solution.py:156
  176.0 4.0 %convolution_add_fusion = f32[256,2048]{1,0:T(8,128)} fusion(f32[256,2048]{1,0:T(8,128)} %fusion.7, bf16[1,2048,256]{2,1,0:T(8,128)(2,1)S(1)} %copy-done.1, bf16[1,1024,256]{2,1,0:T(8,128)(2,1)} %param.19, f32[1024]{0:T(1024)S(1)} %copy-done.13, f32[256,1024]{1,0:T(8,128)S(1)} %get-tuple-element.35, f32[1024]{0:T(1024)S(1)} %get-tuple-element.34), kind=kOutput, calls=%fused_computation | convolution fusion | flops 404029440 | bytes 6823936 | tf_op jit(solution)/shard_map/dot_general | solution.py:159
  180.0 54.5 %all_to_all.78 = f32[16,16,2048]{2,1,0:T(8,128)S(1)} all-to-all(f32[16,16,2048]{2,1,0:T(8,128)} %bitcast.85), channel_id=1, replica_groups=mesh['section'=16,'tensor'=16,'dp'=2] {'tensor'}, dimensions={0} | all-to-all | bytes 4194304 | tf_op jit(solution)/shard_map/all_to_all | solution.py:54
  234.7 15.3 %all_to_all.79 = f32[16,16,128]{2,1,0:T(8,128)S(1)} all-to-all(f32[16,16,128]{2,1,0:T(8,128)S(1)} %copy.28), channel_id=1, replica_groups=mesh['section'=16,'tensor'=16,'dp'=2] {'section'}, dimensions={0} | all-to-all | bytes 262144 | tf_op jit(solution)/shard_map/all_to_all | solution.py:54
  250.2 9.4 %all_to_all.80 = f32[16,1,16]{2,1,0:T(1,128)S(1)} all-to-all(f32[16,1,16]{2,1,0:T(1,128)S(1)} %broadcast_in_dim.43), channel_id=1, replica_groups=mesh['section'=16,'tensor'=16,'dp'=2] {'section'}, dimensions={0} | all-to-all | bytes 2048 | tf_op jit(solution)/shard_map/all_to_all | solution.py:29
  259.7 0.8 fusion.39
  260.4 11.9 %all_to_all.81 = bf16[16,16,128]{2,1,0:T(8,128)(2,1)S(1)} all-to-all(bf16[16,16,128]{2,1,0:T(8,128)(2,1)S(1)} %broadcast_in_dim.44), channel_id=1, replica_groups=mesh['section'=16,'tensor'=16,'dp'=2] {'tensor'}, dimensions={0} | all-to-all | bytes 131072 | tf_op jit(solution)/shard_map/all_to_all | solution.py:29
  272.3 1.9 fusion.26
  274.2 5.6 %all-to-all-start.11 = ((f32[16,16,512]{2,1,0:T(8,128)}), f32[16,16,512]{2,1,0:T(8,128)S(1)}, u32[]{:S(2)}, u32[]{:S(2)}) async-start(f32[16,16,512]{2,1,0:T(8,128)} %fusion.26), calls=%async_computation.11 | async-start | bytes 1048576 | tf_op jit(solution)/shard_map/all_to_all | solution.py:54
  280.2 1.0 copy.31
  281.2 16.0 %all-to-all-done.11 = f32[16,16,512]{2,1,0:T(8,128)S(1)} async-done(((f32[16,16,512]{2,1,0:T(8,128)}), f32[16,16,512]{2,1,0:T(8,128)S(1)}, u32[]{:S(2)}, u32[]{:S(2)}) %all-to-all-start.11) | async-done | bytes 524320 | tf_op jit(solution)/shard_map/all_to_all | solution.py:54
  297.3 15.9 %all_gather.3 = bf16[256,1024]{1,0:T(8,128)(2,1)S(1)} all-gather(bf16[16,1024]{1,0:T(8,128)(2,1)S(1)} %pad_maximum_fusion.1), channel_id=1, replica_groups=mesh['section'=16,'tensor'=16,'dp'=2] {'section'}, dimensions={0}, use_global_device_ids=true | all-gather | bytes 557056 | tf_op jit(solution)/shard_map/all_gather | solution.py:64
  313.4 0.9 convolution_add_fusion.1
  314.3 3.5 %all-to-all-start.12 = ((f32[16,16,128]{2,1,0:T(8,128)}), f32[16,16,128]{2,1,0:T(8,128)S(1)}, u32[]{:S(2)}, u32[]{:S(2)}) async-start(f32[16,16,128]{2,1,0:T(8,128)} %bitcast.19), calls=%async_computation.12 | async-start | bytes 262144 | tf_op jit(solution)/shard_map/all_to_all | solution.py:54
  317.8 0.9 fusion.6
  318.8 0.9 convolution_convert_fusion.4
  319.6 6.4 %all-to-all-done.12 = f32[16,16,128]{2,1,0:T(8,128)S(1)} async-done(((f32[16,16,128]{2,1,0:T(8,128)}), f32[16,16,128]{2,1,0:T(8,128)S(1)}, u32[]{:S(2)}, u32[]{:S(2)}) %all-to-all-start.12) | async-done | bytes 131104 | tf_op jit(solution)/shard_map/all_to_all | solution.py:54
  326.2 0.6 broadcast_in_dim.45
  326.8 6.2 %all-to-all-start.13 = ((f32[16,1,16]{2,1,0:T(1,128)}), f32[16,1,16]{2,1,0:T(1,128)S(1)}, u32[]{:S(2)}, u32[]{:S(2)}) async-start(f32[16,1,16]{2,1,0:T(1,128)} %broadcast_in_dim.45), calls=%async_computation.13 | async-start | bytes 16384 | tf_op jit(solution)/shard_map/all_to_all | solution.py:29
  333.0 0.9 convolution_convert_fusion.3
  333.9 6.1 %all-to-all-done.13 = f32[16,1,16]{2,1,0:T(1,128)S(1)} async-done(((f32[16,1,16]{2,1,0:T(1,128)}), f32[16,1,16]{2,1,0:T(1,128)S(1)}, u32[]{:S(2)}, u32[]{:S(2)}) %all-to-all-start.13) | async-done | bytes 1056 | tf_op jit(solution)/shard_map/all_to_all | solution.py:29
  340.0 0.7 fusion.36
  (101 shorter events, 4.5 us)
Async XLA Ops:
  0.6 168.5 %copy-start = (bf16[1,2048,256]{2,1,0:T(8,128)(2,1)S(1)}, bf16[1,2048,256]{2,1,0:T(8,128)(2,1)}, u32[]{:S(2)}) copy-start(bf16[1,2048,256]{2,1,0:T(8,128)(2,1)} %param.16) | copy-start | bytes 3145732
  20.2 0.5 copy-start.19
  38.1 48.5 %copy-start.9 = (bf16[512,128]{1,0:T(8,128)(2,1)S(1)}, bf16[512,128]{1,0:T(8,128)(2,1)}, u32[]{:S(2)}) copy-start(bf16[512,128]{1,0:T(8,128)(2,1)} %param.15) | copy-start | bytes 393220
  71.3 28.8 %copy-start.11 = (bf16[16,128]{1,0:T(8,128)(2,1)S(1)}, bf16[16,128]{1,0:T(8,128)(2,1)}, u32[]{:S(2)}) copy-start(bf16[16,128]{1,0:T(8,128)(2,1)} %param.10) | copy-start | bytes 12292
  71.3 40.2 %copy-start.14 = (f32[128]{0:T(128)S(1)}, f32[128]{0:T(128)}, u32[]{:S(2)}) copy-start(f32[128]{0:T(128)} %param.12) | copy-start | bytes 1540
  85.8 0.7 copy-start.5
  87.5 12.6 %all-to-all-start.4 = ((f32[16,16,128]{2,1,0:T(8,128)}), f32[16,16,128]{2,1,0:T(8,128)S(1)}, u32[]{:S(2)}, u32[]{:S(2)}) async-start(f32[16,16,128]{2,1,0:T(8,128)} %fusion.28), calls=%async_computation.4 | async-start | bytes 262144 | tf_op jit(solution)/shard_map/all_to_all | solution.py:54
  100.8 10.7 %all-to-all-start.5 = ((f32[16,1,16]{2,1,0:T(1,128)}), f32[16,1,16]{2,1,0:T(1,128)S(1)}, u32[]{:S(2)}, u32[]{:S(2)}) async-start(f32[16,1,16]{2,1,0:T(1,128)} %broadcast_in_dim.41), calls=%async_computation.5 | async-start | bytes 16384 | tf_op jit(solution)/shard_map/all_to_all | solution.py:29
  111.5 38.0 %copy-start.16 = (f32[16]{0:T(128)}, f32[16]{0:T(128)S(1)}, u32[]{:S(2)}) copy-start(f32[16]{0:T(128)S(1)} %add_rsqrt_fusion) | copy-start | bytes 196
  111.6 1.6 collective-permute-start
  112.4 3.3 collective-permute-start.1
  113.2 4.0 %collective-permute-start.2 = (bf16[16,128]{1,0:T(8,128)(2,1)S(1)}, bf16[16,128]{1,0:T(8,128)(2,1)S(1)}, u32[]{:S(2)}, u32[]{:S(2)}) collective-permute-start(bf16[16,128]{1,0:T(8,128)(2,1)S(1)} %collective-permute-done), channel_id=1, source_target_pairs={{0,32},{32,64},{64,96},{96,128},{128,160},{160,192},{192,224},{224... | collective-permute-start | bytes 12296 | tf_op jit(solution)/shard_map/ppermute | solution.py:17
  115.8 3.0 collective-permute-start.3
  117.2 4.2 %collective-permute-start.4 = (bf16[16,128]{1,0:T(8,128)(2,1)S(1)}, bf16[16,128]{1,0:T(8,128)(2,1)S(1)}, u32[]{:S(2)}, u32[]{:S(2)}) collective-permute-start(bf16[16,128]{1,0:T(8,128)(2,1)S(1)} %collective-permute-done.2), channel_id=1, source_target_pairs={{0,32},{32,64},{64,96},{96,128},{128,160},{160,192},{192,224},{224... | collective-permute-start | bytes 12296 | tf_op jit(solution)/shard_map/ppermute | solution.py:17
  118.8 3.0 collective-permute-start.5
  121.4 4.2 %collective-permute-start.6 = (bf16[16,128]{1,0:T(8,128)(2,1)S(1)}, bf16[16,128]{1,0:T(8,128)(2,1)S(1)}, u32[]{:S(2)}, u32[]{:S(2)}) collective-permute-start(bf16[16,128]{1,0:T(8,128)(2,1)S(1)} %collective-permute-done.4), channel_id=1, source_target_pairs={{0,32},{32,64},{64,96},{96,128},{128,160},{160,192},{192,224},{224... | collective-permute-start | bytes 12296 | tf_op jit(solution)/shard_map/ppermute | solution.py:17
  121.8 4.0 %collective-permute-start.7 = (bf16[16,128]{1,0:T(8,128)(2,1)S(1)}, bf16[16,128]{1,0:T(8,128)(2,1)S(1)}, u32[]{:S(2)}, u32[]{:S(2)}) collective-permute-start(bf16[16,128]{1,0:T(8,128)(2,1)S(1)} %collective-permute-done.5), channel_id=1, source_target_pairs={{0,480},{32,0},{64,32},{96,64},{128,96},{160,128},{192,160},{224,1... | collective-permute-start | bytes 12296 | tf_op jit(solution)/shard_map/ppermute | solution.py:20
  125.7 4.2 %collective-permute-start.8 = (bf16[16,128]{1,0:T(8,128)(2,1)S(1)}, bf16[16,128]{1,0:T(8,128)(2,1)S(1)}, u32[]{:S(2)}, u32[]{:S(2)}) collective-permute-start(bf16[16,128]{1,0:T(8,128)(2,1)S(1)} %collective-permute-done.6), channel_id=1, source_target_pairs={{0,32},{32,64},{64,96},{96,128},{128,160},{160,192},{192,224},{224... | collective-permute-start | bytes 12296 | tf_op jit(solution)/shard_map/ppermute | solution.py:17
  125.9 4.2 %collective-permute-start.9 = (bf16[16,128]{1,0:T(8,128)(2,1)S(1)}, bf16[16,128]{1,0:T(8,128)(2,1)S(1)}, u32[]{:S(2)}, u32[]{:S(2)}) collective-permute-start(bf16[16,128]{1,0:T(8,128)(2,1)S(1)} %collective-permute-done.7), channel_id=1, source_target_pairs={{0,480},{32,0},{64,32},{96,64},{128,96},{160,128},{192,160},{224,1... | collective-permute-start | bytes 12296 | tf_op jit(solution)/shard_map/ppermute | solution.py:20
  129.9 4.2 %collective-permute-start.10 = (bf16[16,128]{1,0:T(8,128)(2,1)S(1)}, bf16[16,128]{1,0:T(8,128)(2,1)S(1)}, u32[]{:S(2)}, u32[]{:S(2)}) collective-permute-start(bf16[16,128]{1,0:T(8,128)(2,1)S(1)} %collective-permute-done.8), channel_id=1, source_target_pairs={{0,32},{32,64},{64,96},{96,128},{128,160},{160,192},{192,224},{224... | collective-permute-start | bytes 12296 | tf_op jit(solution)/shard_map/ppermute | solution.py:17
  130.1 4.2 %collective-permute-start.11 = (bf16[16,128]{1,0:T(8,128)(2,1)S(1)}, bf16[16,128]{1,0:T(8,128)(2,1)S(1)}, u32[]{:S(2)}, u32[]{:S(2)}) collective-permute-start(bf16[16,128]{1,0:T(8,128)(2,1)S(1)} %collective-permute-done.9), channel_id=1, source_target_pairs={{0,480},{32,0},{64,32},{96,64},{128,96},{160,128},{192,160},{224,1... | collective-permute-start | bytes 12296 | tf_op jit(solution)/shard_map/ppermute | solution.py:20
  134.2 4.2 %collective-permute-start.12 = (bf16[16,128]{1,0:T(8,128)(2,1)S(1)}, bf16[16,128]{1,0:T(8,128)(2,1)S(1)}, u32[]{:S(2)}, u32[]{:S(2)}) collective-permute-start(bf16[16,128]{1,0:T(8,128)(2,1)S(1)} %collective-permute-done.10), channel_id=1, source_target_pairs={{0,32},{32,64},{64,96},{96,128},{128,160},{160,192},{192,224},{224... | collective-permute-start | bytes 12296 | tf_op jit(solution)/shard_map/ppermute | solution.py:17
  134.4 4.2 %collective-permute-start.13 = (bf16[16,128]{1,0:T(8,128)(2,1)S(1)}, bf16[16,128]{1,0:T(8,128)(2,1)S(1)}, u32[]{:S(2)}, u32[]{:S(2)}) collective-permute-start(bf16[16,128]{1,0:T(8,128)(2,1)S(1)} %collective-permute-done.11), channel_id=1, source_target_pairs={{0,480},{32,0},{64,32},{96,64},{128,96},{160,128},{192,160},{224,1... | collective-permute-start | bytes 12296 | tf_op jit(solution)/shard_map/ppermute | solution.py:20
  138.4 4.2 %collective-permute-start.14 = (bf16[16,128]{1,0:T(8,128)(2,1)S(1)}, bf16[16,128]{1,0:T(8,128)(2,1)S(1)}, u32[]{:S(2)}, u32[]{:S(2)}) collective-permute-start(bf16[16,128]{1,0:T(8,128)(2,1)S(1)} %collective-permute-done.12), channel_id=1, source_target_pairs={{0,32},{32,64},{64,96},{96,128},{128,160},{160,192},{192,224},{224... | collective-permute-start | bytes 12296 | tf_op jit(solution)/shard_map/ppermute | solution.py:17
  142.7 26.1 %copy-start.1 = (bf16[1,2048,256]{2,1,0:T(8,128)(2,1)S(1)}, bf16[1,2048,256]{2,1,0:T(8,128)(2,1)}, u32[]{:S(2)}) copy-start(bf16[1,2048,256]{2,1,0:T(8,128)(2,1)} %param.17) | copy-start | bytes 3145732
  143.8 25.0 %all-to-all-start.6 = ((bf16[16,16,2048]{2,1,0:T(8,128)(2,1)}), bf16[16,16,2048]{2,1,0:T(8,128)(2,1)S(1)}, u32[]{:S(2)}, u32[]{:S(2)}) async-start(bf16[16,16,2048]{2,1,0:T(8,128)(2,1)} %broadcast_in_dim.42), calls=%async_computation.6 | async-start | bytes 2097152 | tf_op jit(solution)/shard_map/all_to_all | solution.py:29
  168.7 1.0 copy-start.2
  169.2 1.1 copy-start.7
  170.3 0.6 copy-start.12
  170.3 1.0 copy-start.3
  172.5 3.5 %copy-start.13 = (f32[1024]{0:T(1024)S(1)}, f32[1024]{0:T(1024)}, u32[]{:S(2)}) copy-start(f32[1024]{0:T(1024)} %copy-done.12) | copy-start | bytes 12292
  234.5 15.5 %copy-start.15 = (f32[128]{0:T(128)S(1)}, f32[128]{0:T(128)}, u32[]{:S(2)}) copy-start(f32[128]{0:T(128)} %param.12) | copy-start | bytes 1540
  234.6 45.2 %copy-start.4 = (bf16[256,1024]{1,0:T(8,128)(2,1)S(1)}, bf16[256,1024]{1,0:T(8,128)(2,1)}, u32[]{:S(2)}) copy-start(bf16[256,1024]{1,0:T(8,128)(2,1)} %fusion.3) | copy-start | bytes 1572868
  274.2 38.9 %copy-start.10 = (bf16[128,512]{1,0:T(8,128)(2,1)S(1)}, bf16[128,512]{1,0:T(8,128)(2,1)}, u32[]{:S(2)}) copy-start(bf16[128,512]{1,0:T(8,128)(2,1)} %param.13) | copy-start | bytes 393220
  274.2 22.9 %all-to-all-start.11 = ((f32[16,16,512]{2,1,0:T(8,128)}), f32[16,16,512]{2,1,0:T(8,128)S(1)}, u32[]{:S(2)}, u32[]{:S(2)}) async-start(f32[16,16,512]{2,1,0:T(8,128)} %fusion.26), calls=%async_computation.11 | async-start | bytes 1048576 | tf_op jit(solution)/shard_map/all_to_all | solution.py:54
  279.8 33.6 %copy-start.8 = (bf16[128,512]{1,0:T(8,128)(2,1)S(1)}, bf16[128,512]{1,0:T(8,128)(2,1)}, u32[]{:S(2)}) copy-start(bf16[128,512]{1,0:T(8,128)(2,1)} %param.14) | copy-start | bytes 393220
  280.2 37.7 %copy-start.6 = (bf16[16,16,512]{2,1,0:T(8,128)(2,1)S(1)}, bf16[16,16,512]{2,1,0:T(8,128)(2,1)}, u32[]{:S(2)}) copy-start(bf16[16,16,512]{2,1,0:T(8,128)(2,1)} %copy-done.5) | copy-start | bytes 786436
  297.2 28.8 %copy-start.18 = (f32[128]{0:T(128)S(1)}, f32[128]{0:T(128)}, u32[]{:S(2)}) copy-start(f32[128]{0:T(128)} %param.11) | copy-start | bytes 1540
  313.2 26.8 %copy-start.17 = (f32[16]{0:T(128)S(1)}, f32[16]{0:T(128)}, u32[]{:S(2)}) copy-start(f32[16]{0:T(128)} %copy-done.16) | copy-start | bytes 196
  313.2 26.8 %copy-start.20 = (f32[16]{0:T(128)S(1)}, f32[16]{0:T(128)}, u32[]{:S(2)}) copy-start(f32[16]{0:T(128)} %copy-done.19) | copy-start | bytes 196
  314.3 11.7 %all-to-all-start.12 = ((f32[16,16,128]{2,1,0:T(8,128)}), f32[16,16,128]{2,1,0:T(8,128)S(1)}, u32[]{:S(2)}, u32[]{:S(2)}) async-start(f32[16,16,128]{2,1,0:T(8,128)} %bitcast.19), calls=%async_computation.12 | async-start | bytes 262144 | tf_op jit(solution)/shard_map/all_to_all | solution.py:54
  326.8 13.2 %all-to-all-start.13 = ((f32[16,1,16]{2,1,0:T(1,128)}), f32[16,1,16]{2,1,0:T(1,128)S(1)}, u32[]{:S(2)}, u32[]{:S(2)}) async-start(f32[16,1,16]{2,1,0:T(1,128)} %broadcast_in_dim.45), calls=%async_computation.13 | async-start | bytes 16384 | tf_op jit(solution)/shard_map/all_to_all | solution.py:29
